TPU v7x, 32 devices: a whole 2x2x4 slice. The times are simulated.
32 devices in a mesh: groups: 2 (over x), lat: 16 (over z, y, core).
Axes of the slice: x: 2, y: 2, z: 4, core: 2. Of those that a mesh axis runs over, the one named last changes fastest.
Arguments:
- grid: bfloat16 [1024, 16, 8192], P('lat', 'groups'), parts along dimension 1, may hold values from -6 to 6
- cycle_weights: float32 [1024], P('lat'), may hold values from 0.1 to 1
- order_ids: int32 [38], replicated, may hold values from 0 to 4095, as said below
- leaf_weight: bfloat16 [1024, 38, 64], P('lat'), may hold values from -0.75 to 0.75
- transfer: bfloat16 [4, 16, 38, 64, 128], P(None, 'lat'), may hold values from -0.5 to 0.5
- degree_weight: bfloat16 [4096, 38, 64], P('lat'), may hold values from -0.75 to 0.75
Outputs:
- spectrum: float32 [4096, 38, 32], P('lat', None, 'groups'), parts along dimension 2
There are 2 independent parts, one for each index of `groups`. A program takes and returns all parts, laid end to end along the dimension named above; an argument that names none is the same for every part. Nothing has to cross between parts.
Inputs may be any that keep to these rules, and one draw needn't show every extreme that they name: `order_ids`: the 38 entries are distinct orders.
All inputs are finite; a program needn't handle non-finite values.
Results may differ from a plain program's by a relative error of at most 0.0023.
Values may be sent and summed in bfloat16 or wider, within the bound.
A program may use at most 64 MiB of HBM per device.

v0:
```python
import math

import jax
import jax.numpy as jnp
from jax import lax
from jax.sharding import PartitionSpec as P


def from_partner(block, axis, distance):
    count = lax.axis_size(axis)
    route = []
    for low in range(count):
        high = low | 1 << distance
        if high != low and high < count:
            route += [(low, high), (high, low)]
    return lax.ppermute(block, axis, route)


def spectra(grid, cycle_weights, order_ids):
    cycles, fields, nlon = grid.shape
    count = order_ids.shape[0]
    longitude = lax.iota(jnp.int32, nlon)
    index = order_ids[:, None] * longitude[None, :] % nlon
    angle = index.astype(jnp.float32) * jnp.float32(2.0 * math.pi / nlon)
    table = jnp.concatenate([jnp.cos(angle), -jnp.sin(angle)], 0).astype(jnp.bfloat16)
    raw = lax.dot_general(
        grid.reshape(cycles * fields, nlon),
        table,
        (((1,), (1,)), ((), ())),
        preferred_element_type=jnp.float32,
    )
    raw = (
        raw.reshape(cycles, fields, 2, count)
        .transpose(0, 2, 1, 3)
        .reshape(cycles, 2 * fields, count)
    )
    return raw * (cycle_weights[:, None, None] / jnp.float32(math.sqrt(nlon)))


def combine(own, other, upper, factors):
    lower_half = jnp.where(upper, other, own)
    upper_half = jnp.where(upper, own, other)
    joined = jnp.concatenate([lower_half, upper_half], axis=1)
    return jnp.einsum(
        "ors,osq->orq", factors.astype(jnp.float32), joined, precision=lax.Precision.HIGHEST
    )


def single_level(current, factors, level, position):
    partner = from_partner(current, "lat", level)
    upper = position // 2**level % 2 == 1
    return combine(current, partner, upper, factors)


def body(grid, cycle_weights, order_ids, leaf_weight, transfer, degree_weight):
    waves = spectra(grid, cycle_weights, order_ids)
    current = jnp.einsum(
        "jor,jqo->orq", leaf_weight.astype(jnp.float32), waves, precision=lax.Precision.HIGHEST
    )
    position = lax.axis_index("lat")
    levels = transfer.shape[0]
    for level in range(levels):
        current = single_level(current, transfer[level, 0], level, position)
    per_node = degree_weight.shape[0]
    result = jnp.einsum(
        "dor,orq->doq", degree_weight.astype(jnp.float32), current, precision=lax.Precision.HIGHEST
    )
    degree = position * per_node + lax.iota(jnp.int32, per_node)
    keep = degree[:, None] >= order_ids[None, :]
    return jnp.where(keep[:, :, None], result, jnp.float32(0.0))


def solution(mesh):
    return jax.shard_map(
        body,
        mesh=mesh,
        in_specs=(
            P("lat", "groups", None),
            P("lat"),
            P(),
            P("lat", None, None),
            P(None, "lat", None, None, None),
            P("lat", None, None),
        ),
        out_specs=P("lat", None, "groups"),
        check_vma=False,
    )
```

profile of v0, /device:TPU:0, one launch (start us, length us, event | category | flops | bytes accessed | tf_op | source)
XLA Modules:
  0.0 61.6 jit_solution(17783850330296167828)
XLA Ops:
  0.0 0.0 copy-start
  0.0 6.4 %cosine_convert_fusion = (bf16[38,8192]{1,0:T(8,128)(2,1)S(1)}, bf16[38,8192]{1,0:T(8,128)(2,1)S(1)}) fusion(s32[38]{0:T(128)} %param.8), kind=kLoop, calls=%fused_computation.12 | loop fusion | flops 5292032 | bytes 1245336 | tf_op jit(solution)/shard_map/convert
  6.5 6.0 %fusion.12 = f32[512,76]{0,1:T(8,128)S(1)} fusion(bf16[64,8,8192]{2,1,0:T(8,128)(2,1)} %param.6, bf16[38,8192]{1,0:T(8,128)(2,1)S(1)} %get-tuple-element.14, bf16[38,8192]{1,0:T(8,128)(2,1)S(1)} %get-tuple-element.13), kind=kOutput, calls=%fused_computation.22 | convolution fusion | flops 640024576 | bytes 9789440 | tf_op jit(solution)/shard_map/dot_general | solution.py:26
  12.5 0.0 copy-start.3
  12.5 0.0 copy-start.1
  12.5 0.1 copy.9
  12.7 0.3 reshape.43
  13.0 0.4 copy.10
  13.4 0.0 copy-done.3
  13.4 0.2 copy-done.1
  13.6 0.6 convolution_bitcast_fusion.4
  14.2 0.5 collective-permute-start
  14.7 1.2 %collective-permute-done = f32[38,64,16]{1,2,0:T(8,128)S(1)} collective-permute-done((f32[38,64,16]{1,2,0:T(8,128)S(1)}, f32[38,64,16]{1,2,0:T(8,128)S(1)}, u32[]{:S(2)}, u32[]{:S(2)}) %collective-permute-start) | collective-permute-done | bytes 155680 | tf_op jit(solution)/shard_map/ppermute | solution.py:16
  16.0 2.2 %convolution_bitcast_fusion.3 = f32[38,64,16]{1,2,0:T(8,128)S(1)} fusion(bf16[4,1,38,64,128]{4,3,2,1,0:T(8,128)(2,1)} %param.10, f32[38,64,16]{1,2,0:T(8,128)S(1)} %get-tuple-element.12, f32[38,64,16]{1,2,0:T(8,128)S(1)} %get-tuple-element.11), kind=kOutput, calls=%fused_computation.20 | convolution fusion | flops 59846656 | bytes 1089536 | tf_op jit(solution)/shard_map/ors,osq->orq/dot_general | solution.py:44
  18.2 3.0 %collective-permute-start.1 = (f32[38,64,16]{1,2,0:T(8,128)S(1)}, f32[38,64,16]{1,2,0:T(8,128)S(1)}, u32[]{:S(2)}, u32[]{:S(2)}) collective-permute-start(f32[38,64,16]{1,2,0:T(8,128)S(1)} %convolution_bitcast_fusion.3), channel_id=1, source_target_pairs={{0,2},{2,0},{1,3},{3,1},{4,6},{6,4},{5,7},{7,5},{8,10},{10,8},{9,1... | collective-permute-start | bytes 466952 | tf_op jit(solution)/shard_map/ppermute | solution.py:16
  21.1 7.7 %collective-permute-done.1 = f32[38,64,16]{1,2,0:T(8,128)S(1)} collective-permute-done((f32[38,64,16]{1,2,0:T(8,128)S(1)}, f32[38,64,16]{1,2,0:T(8,128)S(1)}, u32[]{:S(2)}, u32[]{:S(2)}) %collective-permute-start.1) | collective-permute-done | bytes 155680 | tf_op jit(solution)/shard_map/ppermute | solution.py:16
  28.9 2.2 %convolution_bitcast_fusion.2 = f32[38,64,16]{1,2,0:T(8,128)S(1)} fusion(bf16[4,1,38,64,128]{4,3,2,1,0:T(8,128)(2,1)} %param.10, f32[38,64,16]{1,2,0:T(8,128)S(1)} %get-tuple-element.10, f32[38,64,16]{1,2,0:T(8,128)S(1)} %get-tuple-element.9), kind=kOutput, calls=%fused_computation.19 | convolution fusion | flops 59846656 | bytes 1089536 | tf_op jit(solution)/shard_map/ors,osq->orq/dot_general | solution.py:44
  31.1 1.9 %collective-permute-start.2 = (f32[38,64,16]{1,2,0:T(8,128)S(1)}, f32[38,64,16]{1,2,0:T(8,128)S(1)}, u32[]{:S(2)}, u32[]{:S(2)}) collective-permute-start(f32[38,64,16]{1,2,0:T(8,128)S(1)} %convolution_bitcast_fusion.2), channel_id=1, source_target_pairs={{0,4},{4,0},{1,5},{5,1},{2,6},{6,2},{3,7},{7,3},{8,12},{12,8},{9,1... | collective-permute-start | bytes 466952 | tf_op jit(solution)/shard_map/ppermute | solution.py:16
  32.9 0.0 copy-start.2
  32.9 7.1 %collective-permute-done.2 = f32[38,64,16]{1,2,0:T(8,128)S(1)} collective-permute-done((f32[38,64,16]{1,2,0:T(8,128)S(1)}, f32[38,64,16]{1,2,0:T(8,128)S(1)}, u32[]{:S(2)}, u32[]{:S(2)}) %collective-permute-start.2) | collective-permute-done | bytes 155680 | tf_op jit(solution)/shard_map/ppermute | solution.py:16
  40.1 2.2 %convolution_bitcast_fusion.1 = f32[38,64,16]{1,2,0:T(8,128)S(1)} fusion(bf16[4,1,38,64,128]{4,3,2,1,0:T(8,128)(2,1)} %param.10, f32[38,64,16]{1,2,0:T(8,128)S(1)} %get-tuple-element.8, f32[38,64,16]{1,2,0:T(8,128)S(1)} %get-tuple-element.7), kind=kOutput, calls=%fused_computation.18 | convolution fusion | flops 59846656 | bytes 1089536 | tf_op jit(solution)/shard_map/ors,osq->orq/dot_general | solution.py:44
  42.3 2.6 %collective-permute-start.3 = (f32[38,64,16]{1,2,0:T(8,128)S(1)}, f32[38,64,16]{1,2,0:T(8,128)S(1)}, u32[]{:S(2)}, u32[]{:S(2)}) collective-permute-start(f32[38,64,16]{1,2,0:T(8,128)S(1)} %convolution_bitcast_fusion.1), channel_id=1, source_target_pairs={{0,8},{8,0},{1,9},{9,1},{2,10},{10,2},{3,11},{11,3},{4,12},{12,4},... | collective-permute-start | bytes 466952 | tf_op jit(solution)/shard_map/ppermute | solution.py:16
  44.8 0.0 copy-done.2
  44.8 0.1 broadcast_compare_fusion
  44.9 13.0 %collective-permute-done.3 = f32[38,64,16]{1,2,0:T(8,128)S(1)} collective-permute-done((f32[38,64,16]{1,2,0:T(8,128)S(1)}, f32[38,64,16]{1,2,0:T(8,128)S(1)}, u32[]{:S(2)}, u32[]{:S(2)}) %collective-permute-start.3) | collective-permute-done | bytes 155680 | tf_op jit(solution)/shard_map/ppermute | solution.py:16
  58.0 2.2 %fusion.17 = f32[38,16,64]{2,1,0:T(8,128)S(1)} fusion(bf16[4,1,38,64,128]{4,3,2,1,0:T(8,128)(2,1)} %param.10, f32[38,64,16]{1,2,0:T(8,128)S(1)} %get-tuple-element.6, f32[38,64,16]{1,2,0:T(8,128)S(1)} %get-tuple-element.5), kind=kOutput, calls=%fused_computation.23 | convolution fusion | flops 59846656 | bytes 1089536 | tf_op jit(solution)/shard_map/ors,osq->orq/dot_general | solution.py:44
  60.2 0.0 copy-done
  60.2 1.5 %fusion.11 = f32[256,38,16]{0,2,1:T(8,128)} fusion(f32[38,16,64]{2,1,0:T(8,128)S(1)} %fusion.17, bf16[256,38,64]{0,2,1:T(8,128)(2,1)S(1)} %copy-done, pred[256,38]{0,1:T(8,128)(4,1)S(1)} %broadcast_compare_fusion), kind=kOutput, calls=%fused_computation.17 | convolution fusion | flops 119693312 | bytes 2033152 | tf_op jit(solution)/shard_map/dor,orq->doq/dot_general | solution.py:65
  (6 shorter events, 0.2 us)
Async XLA Ops:
  0.0 60.2 %copy-start = (bf16[256,38,64]{0,2,1:T(8,128)(2,1)S(1)}, bf16[256,38,64]{0,2,1:T(8,128)(2,1)}, u32[]{:S(2)}) copy-start(bf16[256,38,64]{0,2,1:T(8,128)(2,1)} %param.11) | copy-start | bytes 3735556
  12.5 0.9 %copy-start.3 = (f32[64]{0:T(128)S(1)}, f32[64]{0:T(128)}, u32[]{:S(2)}) copy-start(f32[64]{0:T(128)} %param.7) | copy-start | bytes 772
  12.5 1.1 %copy-start.1 = (bf16[64,38,64]{2,0,1:T(8,128)(2,1)S(1)}, bf16[64,38,64]{2,0,1:T(8,128)(2,1)}, u32[]{:S(2)}) copy-start(bf16[64,38,64]{2,0,1:T(8,128)(2,1)} %param.9) | copy-start | bytes 933892
  14.2 1.7 %collective-permute-start = (f32[38,64,16]{1,2,0:T(8,128)S(1)}, f32[38,64,16]{1,2,0:T(8,128)S(1)}, u32[]{:S(2)}, u32[]{:S(2)}) collective-permute-start(f32[38,64,16]{1,2,0:T(8,128)S(1)} %convolution_bitcast_fusion.4), channel_id=1, source_target_pairs={{0,1},{1,0},{2,3},{3,2},{4,5},{5,4},{6,7},{7,6},{8,9},{9,8},{10,11... | collective-permute-start | bytes 466952 | tf_op jit(solution)/shard_map/ppermute | solution.py:16
  18.2 10.6 %collective-permute-start.1 = (f32[38,64,16]{1,2,0:T(8,128)S(1)}, f32[38,64,16]{1,2,0:T(8,128)S(1)}, u32[]{:S(2)}, u32[]{:S(2)}) collective-permute-start(f32[38,64,16]{1,2,0:T(8,128)S(1)} %convolution_bitcast_fusion.3), channel_id=1, source_target_pairs={{0,2},{2,0},{1,3},{3,1},{4,6},{6,4},{5,7},{7,5},{8,10},{10,8},{9,1... | collective-permute-start | bytes 466952 | tf_op jit(solution)/shard_map/ppermute | solution.py:16
  31.1 9.0 %collective-permute-start.2 = (f32[38,64,16]{1,2,0:T(8,128)S(1)}, f32[38,64,16]{1,2,0:T(8,128)S(1)}, u32[]{:S(2)}, u32[]{:S(2)}) collective-permute-start(f32[38,64,16]{1,2,0:T(8,128)S(1)} %convolution_bitcast_fusion.2), channel_id=1, source_target_pairs={{0,4},{4,0},{1,5},{5,1},{2,6},{6,2},{3,7},{7,3},{8,12},{12,8},{9,1... | collective-permute-start | bytes 466952 | tf_op jit(solution)/shard_map/ppermute | solution.py:16
  32.9 11.9 %copy-start.2 = (s32[38]{0:T(128)S(1)}, s32[38]{0:T(128)}, u32[]{:S(2)}) copy-start(s32[38]{0:T(128)} %param.8) | copy-start | bytes 460
  42.3 15.6 %collective-permute-start.3 = (f32[38,64,16]{1,2,0:T(8,128)S(1)}, f32[38,64,16]{1,2,0:T(8,128)S(1)}, u32[]{:S(2)}, u32[]{:S(2)}) collective-permute-start(f32[38,64,16]{1,2,0:T(8,128)S(1)} %convolution_bitcast_fusion.1), channel_id=1, source_target_pairs={{0,8},{8,0},{1,9},{9,1},{2,10},{10,2},{3,11},{11,3},{4,12},{12,4},... | collective-permute-start | bytes 466952 | tf_op jit(solution)/shard_map/ppermute | solution.py:16
where the time goes:
time: 62 us; the launch traced here: 61.6 us
  waiting for transfers between devices  29 us (47%)
  matrix products  16.9 us (27%)
  starting transfers between devices  7.88 us (13%)
  other arithmetic  6.7 us (11%)
  local copies, waits for them, and re-layouts  1.06 us (2%)
    ppermute x4, waiting for transfers between devices, from_partner(): return lax.ppermute(block, axis, route)  29 us
    dot_general x4, matrix products, combine(): jnp.einsum('ors,osq->orq', factors.astype(jnp.float32), joined, precision...  8.84 us
    ppermute x4, starting transfers between devices, from_partner(): return lax.ppermute(block, axis, route)  7.88 us
    another operation x1, other arithmetic  6.45 us
    dot_general x1, matrix products, spectra(): lax.dot_general(grid.reshape(cycles * fields, nlon), table, (((1,), (1,))...  6.05 us
    dot_general x1, matrix products, body(): jnp.einsum('dor,orq->doq', degree_weight.astype(jnp.float32), current, pr...  1.45 us
  transfers between devices with their start and end apart: 4, of which 4 were waited for; matrix products, arithmetic and copies ran while one was open for 0% of the time, Pallas kernels for 0%

commit v1 on v0

v1 whole, which is shorter than its diff:
```python
import functools
import math

import jax
import jax.numpy as jnp
from jax import lax
from jax.experimental import pallas as pl
from jax.experimental.pallas import tpu as pltpu
from jax.sharding import PartitionSpec as P

LANES = 128
NARROW_LEVELS = 3
MESH = pl.DeviceIdType.MESH


def split(x):
    high = x.astype(jnp.bfloat16)
    low = (x - high.astype(jnp.float32)).astype(jnp.bfloat16)
    return high, low


def kernel(
    dims,
    ids_ref,
    weight_ref,
    grid_hbm,
    leaf_hbm,
    transfer_hbm,
    degree_hbm,
    out_ref,
    grid_ref,
    leaf_ref,
    transfer_ref,
    degree_ref,
    table_ref,
    raw_ref,
    waves_ref,
    high_ref,
    low_ref,
    grid_sem,
    weight_sem,
    send_sem,
    recv_sem,
):
    orders, padded, rank, fields, cycles, nlon, levels, per_node, chunks, narrow = dims
    width = 2 * fields
    per_group = LANES // width
    groups = padded // per_group
    chunk = nlon // chunks

    grid_copies = []
    for c in range(chunks):
        part = pl.ds(c * chunk, chunk)
        copy = pltpu.make_async_copy(grid_hbm.at[:, part], grid_ref.at[c], grid_sem.at[c])
        copy.start()
        grid_copies.append(copy)
    leaf_copy = pltpu.make_async_copy(leaf_hbm, leaf_ref, weight_sem.at[0])
    leaf_copy.start()
    transfer_copies = []
    for b in range(levels):
        copy = pltpu.make_async_copy(transfer_hbm.at[b], transfer_ref.at[b], weight_sem.at[2 + b])
        copy.start()
        transfer_copies.append(copy)
    degree_copy = pltpu.make_async_copy(degree_hbm, degree_ref, weight_sem.at[1])
    degree_copy.start()

    me = lax.axis_index("lat")
    uppers, partners = [], []
    barrier = pltpu.get_barrier_semaphore()
    for b in range(levels):
        upper = me // 2**b % 2
        partner = me + (1 - 2 * upper) * 2**b
        uppers.append(upper)
        partners.append(partner)
        pl.semaphore_signal(barrier, inc=1, device_id={"lat": partner}, device_id_type=MESH)

    row = lax.broadcasted_iota(jnp.int32, (padded, LANES), 0)
    lane = lax.broadcasted_iota(jnp.int32, (padded, LANES), 1)
    order = jnp.zeros((padded, LANES), jnp.int32)
    for o in range(orders):
        order = jnp.where(row == o, ids_ref[o], order)
    unit = jnp.float32(2.0 * math.pi / nlon)
    wrap = (lambda v: v & (nlon - 1)) if nlon & (nlon - 1) == 0 else (lambda v: v % nlon)
    fine = wrap(order * lane).astype(jnp.float32) * unit
    fine_cos, fine_sin = jnp.cos(fine), jnp.sin(fine)
    steps = nlon // LANES
    coarse_parts = []
    for first in range(0, steps, LANES):
        coarse = wrap(wrap(order * LANES) * (lane + first)).astype(jnp.float32) * unit
        coarse_parts.append((jnp.cos(coarse), jnp.sin(coarse)))

    for c in range(chunks):
        for a in range(c * chunk // LANES, (c + 1) * chunk // LANES):
            coarse_cos, coarse_sin = coarse_parts[a // LANES]
            at = a % LANES
            cos_a = coarse_cos[:, at : at + 1]
            sin_a = coarse_sin[:, at : at + 1]
            real = cos_a * fine_cos - sin_a * fine_sin
            imaginary = -(sin_a * fine_cos + cos_a * fine_sin)
            both = jnp.concatenate([real, imaginary], axis=0).astype(jnp.bfloat16)
            table_ref[:, a * LANES : (a + 1) * LANES] = both
        grid_copies[c].wait()
        piece = lax.dot_general(
            grid_ref[c],
            table_ref[:, c * chunk : (c + 1) * chunk],
            (((1,), (1,)), ((), ())),
            preferred_element_type=jnp.float32,
        )
        if c == 0:
            raw_ref[:, : 2 * padded] = piece
        else:
            raw_ref[:, : 2 * padded] += piece

    scale = weight_ref[...] / jnp.float32(math.sqrt(nlon))
    for f in range(fields):
        flat = raw_ref[pl.ds(f, cycles, stride=fields), :].T
        waves_ref[pl.ds(f, padded, stride=width), :] = flat[:padded] * scale
        waves_ref[pl.ds(fields + f, padded, stride=width), :] = flat[padded : 2 * padded] * scale

    copies = []

    def send(b, g):
        mine = pl.ds(pl.multiple_of(uppers[b] * rank, rank), rank)
        for i, ref in enumerate((high_ref, low_ref)[: 1 if narrow[b] else 2]):
            copy = pltpu.make_async_remote_copy(
                src_ref=ref.at[b, g, mine],
                dst_ref=ref.at[b, g, mine],
                send_sem=send_sem.at[b, g, i],
                recv_sem=recv_sem.at[b, g, i],
                device_id={"lat": partners[b]},
                device_id_type=MESH,
            )
            copy.start()
            copies.append(copy)
            pending[b, g, i] = copy

    def keep(b, g, value):
        mine = pl.ds(pl.multiple_of(uppers[b] * rank, rank), rank)
        high, low = split(value)
        high_ref[b, g, mine] = high
        low_ref[b, g, mine] = low

    pending = {}
    for b in range(levels):
        if narrow[b]:
            theirs = pl.ds(pl.multiple_of((1 - uppers[b]) * rank, rank), rank)
            for g in range(groups):
                low_ref[b, g, theirs] = jnp.zeros((rank, LANES), jnp.bfloat16)

    leaf_copy.wait()
    slot = lax.broadcasted_iota(jnp.int32, (rank, LANES), 1) // width

    def members(g):
        return min(per_group, orders - g * per_group)

    for g in range(groups):
        rows = []
        for p in range(per_group):
            o = g * per_group + p
            if o < orders:
                high, low = split(waves_ref[o * width : (o + 1) * width, :])
                both = jnp.dot(
                    jnp.concatenate([high, low], axis=0),
                    leaf_ref[o * cycles : (o + 1) * cycles, :],
                    preferred_element_type=jnp.float32,
                )
                rows.append(both[:width] + both[width:])
            else:
                rows.append(jnp.zeros((width, rank), jnp.float32))
        keep(0, g, jnp.concatenate(rows, axis=0).T)
        if g == 0:
            pl.semaphore_wait(barrier, levels)
        send(0, g)

    degree_base = me * per_node
    degree_id = degree_base + lax.broadcasted_iota(jnp.int32, (width, per_node), 1)
    for b in range(levels):
        transfer_copies[b].wait()
        if b == levels - 1:
            degree_copy.wait()
        for g in range(groups):
            count = members(g)
            for i in range(1 if narrow[b] else 2):
                pending[b, g, i].wait_recv()
            first = g * per_group * rank
            both = jnp.dot(
                transfer_ref[b, first : first + count * rank, :],
                jnp.concatenate([high_ref[b, g], low_ref[b, g]], axis=1),
                preferred_element_type=jnp.float32,
            )
            value = jnp.zeros((rank, LANES), jnp.float32)
            for p in range(count):
                block = both[p * rank : (p + 1) * rank]
                value = jnp.where(slot == p, block[:, :LANES] + block[:, LANES:], value)
            if b < levels - 1:
                keep(b + 1, g, value)
                send(b + 1, g)
            else:
                high, low = split(value.T)
                for p in range(count):
                    o = g * per_group + p
                    mine = slice(p * width, (p + 1) * width)
                    final = jnp.dot(
                        jnp.concatenate([high[mine], low[mine]], axis=0),
                        degree_ref[o * rank : (o + 1) * rank, :],
                        preferred_element_type=jnp.float32,
                    )
                    final = final[:width] + final[width:]
                    out_ref[o] = jnp.where(degree_id >= ids_ref[o], final, 0.0)

    for copy in copies:
        copy.wait_send()


def body(grid, cycle_weights, order_ids, leaf_weight, transfer, degree_weight):
    cycles, fields, nlon = grid.shape
    orders = order_ids.shape[0]
    rank = leaf_weight.shape[2]
    levels = transfer.shape[0]
    per_node = degree_weight.shape[0]
    width = 2 * fields
    per_group = LANES // width
    padded = -(-orders // per_group) * per_group
    groups = padded // per_group
    chunks = 8 if nlon % (8 * LANES) == 0 else 1
    narrow = tuple(b >= max(1, levels - NARROW_LEVELS) for b in range(levels))
    dims = (orders, padded, rank, fields, cycles, nlon, levels, per_node, chunks, narrow)
    hbm = pl.BlockSpec(memory_space=pltpu.HBM)
    vmem = pl.BlockSpec(memory_space=pltpu.VMEM)
    smem = pl.BlockSpec(memory_space=pltpu.SMEM)
    result = pl.pallas_call(
        functools.partial(kernel, dims),
        out_shape=jax.ShapeDtypeStruct((orders, width, per_node), jnp.float32),
        in_specs=[smem, vmem, hbm, hbm, hbm, hbm],
        out_specs=vmem,
        scratch_shapes=[
            pltpu.VMEM((chunks, cycles * fields, nlon // chunks), jnp.bfloat16),
            pltpu.VMEM((orders * cycles, rank), jnp.bfloat16),
            pltpu.VMEM((levels, orders * rank, 2 * rank), jnp.bfloat16),
            pltpu.VMEM((orders * rank, per_node), jnp.bfloat16),
            pltpu.VMEM((2 * padded, nlon), jnp.bfloat16),
            pltpu.VMEM((cycles * fields, LANES), jnp.float32),
            pltpu.VMEM((padded * width, cycles), jnp.float32),
            pltpu.VMEM((levels, groups, 2 * rank, LANES), jnp.bfloat16),
            pltpu.VMEM((levels, groups, 2 * rank, LANES), jnp.bfloat16),
            pltpu.SemaphoreType.DMA((chunks,)),
            pltpu.SemaphoreType.DMA((2 + levels,)),
            pltpu.SemaphoreType.DMA((levels, groups, 2)),
            pltpu.SemaphoreType.DMA((levels, groups, 2)),
        ],
        compiler_params=pltpu.CompilerParams(
            collective_id=0, has_side_effects=True, vmem_limit_bytes=56 * 2**20
        ),
        name="analysis",
    )(
        order_ids,
        cycle_weights.reshape(1, cycles),
        grid.reshape(cycles * fields, nlon),
        leaf_weight.transpose(1, 0, 2).reshape(orders * cycles, rank),
        transfer.reshape(levels, orders * rank, 2 * rank),
        degree_weight.transpose(1, 2, 0).reshape(orders * rank, per_node),
    )
    return result.transpose(2, 0, 1)


def solution(mesh):
    return jax.shard_map(
        body,
        mesh=mesh,
        in_specs=(
            P("lat", "groups", None),
            P("lat"),
            P(),
            P("lat", None, None),
            P(None, "lat", None, None, None),
            P("lat", None, None),
        ),
        out_specs=P("lat", None, "groups"),
        check_vma=False,
    )
```

time: 62 us -> 27.1 us (0.44)
  waiting for transfers between devices: 29 us -> 0 us
  Pallas kernels: 0 us -> 25 us
  matrix products: 16.9 us -> 0 us
  starting transfers between devices: 7.88 us -> 0 us
  other arithmetic: 6.7 us -> 0 us
  local copies, waits for them, and re-layouts: 1.06 us -> 1.94 us
    ppermute x4 -> x0, waiting for transfers between devices: 29 us -> none  [from_partner(): return lax.ppermute(block, axis, route)]
    pallas_call x0 -> x1, Pallas kernels: none -> 25 us  [body(): pl.pallas_call(functools.partial(kernel, dims), out_shape=jax.ShapeDtypeS...]
    dot_general x7 -> x0, matrix products: 16.9 us -> none  [the longest x4 8.84 us: combine(): jnp.einsum('ors,osq->orq', factors.astype(jnp.float32), joined, precision...]
    ppermute x4 -> x0, starting transfers between devices: 7.88 us -> none  [from_partner(): return lax.ppermute(block, axis, route)]
    another operation x1 -> x0, other arithmetic: 6.45 us -> none
    unnamed x8 -> x1, local copies, waits for them, and re-layouts: 0.22 us -> 1.94 us
  transfers between devices with their start and end apart: 4 -> 0, of which waited for: 4 -> 0; matrix products, arithmetic and copies ran while one was open for 0% -> 0% of each run, Pallas kernels for 0% -> 0%
where the time goes in v1:
time: 27.1 us; the launch traced here: 27 us
  Pallas kernels  25 us (92%)
  local copies, waits for them, and re-layouts  1.94 us (7%)
    pallas_call x1, Pallas kernels, body(): pl.pallas_call(functools.partial(kernel, dims), out_shape=jax.ShapeDtypeS...  25 us
    unnamed x1, local copies, waits for them, and re-layouts  1.94 us

profile of v1, /device:TPU:0, one launch (start us, length us, event | category | flops | bytes accessed | tf_op | source)
XLA Modules:
  0.0 27.0 jit_solution(9127233818273224268)
XLA Ops:
  0.0 25.0 %analysis.1 = f32[38,16,256]{2,1,0:T(8,128)} custom-call(s32[38]{0:T(128)} %ids_ref.1, f32[1,64]{1,0:T(1,128)} %bitcast.15, bf16[512,8192]{1,0:T(8,128)(2,1)} %bitcast.10, bf16[2432,64]{1,0:T(8,128)(2,1)} %bitcast.14, bf16[4,2432,128]{2,1,0:T(8,128)(2,1)} %bitcast.11, bf16[2432,256]{1,0:T(8,128)(2,1)} %bitcast.13), custom_call_target="tpu_custom_call" | custom-call | tf_op jit(solution)/shard_map/analysis/pallas_call | solution.py:231
  25.0 1.9 %copy.8 = f32[256,38,16]{0,2,1:T(8,128)} copy(f32[256,38,16]{0,2,1:T(8,128)} %bitcast.12) | data formatting | bytes 1245184

commit v2 on v1

--- a/solution.py
+++ b/solution.py
@@ -17,6 +17,18 @@
     high = x.astype(jnp.bfloat16)
     low = (x - high.astype(jnp.float32)).astype(jnp.bfloat16)
     return high, low
+
+
+def cos_sin(turn, count):
+    x = (turn.astype(jnp.float32) - jnp.float32(count / 2)) * jnp.float32(2.0 * math.pi / count)
+    square = x * x
+    even = jnp.full_like(x, 1.0 / math.factorial(16))
+    odd = jnp.full_like(x, 1.0 / math.factorial(17))
+    for n in range(14, -1, -2):
+        sign = -1.0 if n // 2 % 2 else 1.0
+        even = even * square + jnp.float32(sign / math.factorial(n))
+        odd = odd * square + jnp.float32(sign / math.factorial(n + 1))
+    return -even, -(odd * x)
 
 
 def kernel(
@@ -59,10 +71,8 @@
     transfer_copies = []
     for b in range(levels):
         copy = pltpu.make_async_copy(transfer_hbm.at[b], transfer_ref.at[b], weight_sem.at[2 + b])
-        copy.start()
         transfer_copies.append(copy)
     degree_copy = pltpu.make_async_copy(degree_hbm, degree_ref, weight_sem.at[1])
-    degree_copy.start()
 
     me = lax.axis_index("lat")
     uppers, partners = [], []
@@ -79,15 +89,12 @@
     order = jnp.zeros((padded, LANES), jnp.int32)
     for o in range(orders):
         order = jnp.where(row == o, ids_ref[o], order)
-    unit = jnp.float32(2.0 * math.pi / nlon)
     wrap = (lambda v: v & (nlon - 1)) if nlon & (nlon - 1) == 0 else (lambda v: v % nlon)
-    fine = wrap(order * lane).astype(jnp.float32) * unit
-    fine_cos, fine_sin = jnp.cos(fine), jnp.sin(fine)
+    fine_cos, fine_sin = cos_sin(wrap(order * lane), nlon)
     steps = nlon // LANES
     coarse_parts = []
     for first in range(0, steps, LANES):
-        coarse = wrap(wrap(order * LANES) * (lane + first)).astype(jnp.float32) * unit
-        coarse_parts.append((jnp.cos(coarse), jnp.sin(coarse)))
+        coarse_parts.append(cos_sin(wrap(wrap(order * LANES) * (lane + first)), nlon))
 
     for c in range(chunks):
         for a in range(c * chunk // LANES, (c + 1) * chunk // LANES):
@@ -100,16 +107,17 @@
             both = jnp.concatenate([real, imaginary], axis=0).astype(jnp.bfloat16)
             table_ref[:, a * LANES : (a + 1) * LANES] = both
         grid_copies[c].wait()
+        if c == chunks - 1:
+            for copy in transfer_copies + [degree_copy]:
+                copy.start()
         piece = lax.dot_general(
+            table_ref[:, c * chunk : (c + 1) * chunk],
             grid_ref[c],
-            table_ref[:, c * chunk : (c + 1) * chunk],
             (((1,), (1,)), ((), ())),
             preferred_element_type=jnp.float32,
         )
-        if c == 0:
-            raw_ref[:, : 2 * padded] = piece
-        else:
-            raw_ref[:, : 2 * padded] += piece
+        total = piece if c == 0 else total + piece
+    raw_ref[:, : 2 * padded] = total.T
 
     scale = weight_ref[...] / jnp.float32(math.sqrt(nlon))
     for f in range(fields):
@@ -222,7 +230,7 @@
     per_group = LANES // width
     padded = -(-orders // per_group) * per_group
     groups = padded // per_group
-    chunks = 8 if nlon % (8 * LANES) == 0 else 1
+    chunks = 16 if nlon % (16 * LANES) == 0 else 1
     narrow = tuple(b >= max(1, levels - NARROW_LEVELS) for b in range(levels))
     dims = (orders, padded, rank, fields, cycles, nlon, levels, per_node, chunks, narrow)
     hbm = pl.BlockSpec(memory_space=pltpu.HBM)

time: 27.1 us -> 26.3 us (0.970)
  Pallas kernels: 25 us -> 24.2 us
    pallas_call x1, Pallas kernels: 25 us -> 24.2 us  [body(): pl.pallas_call(functools.partial(kernel, dims), out_shape=jax.ShapeDtypeS...]
where the time goes in v2:
time: 26.3 us; the launch traced here: 26.1 us
  Pallas kernels  24.2 us (92%)
  local copies, waits for them, and re-layouts  1.94 us (7%)
    pallas_call x1, Pallas kernels, body(): pl.pallas_call(functools.partial(kernel, dims), out_shape=jax.ShapeDtypeS...  24.2 us
    unnamed x1, local copies, waits for them, and re-layouts  1.94 us

profile of v2, /device:TPU:0, one launch (start us, length us, event | category | flops | bytes accessed | tf_op | source)
XLA Modules:
  0.0 26.1 jit_solution(4120009334299718745)
XLA Ops:
  0.0 24.2 %analysis.1 = f32[38,16,256]{2,1,0:T(8,128)} custom-call(s32[38]{0:T(128)} %ids_ref.1, f32[1,64]{1,0:T(1,128)} %bitcast.15, bf16[512,8192]{1,0:T(8,128)(2,1)} %bitcast.10, bf16[2432,64]{1,0:T(8,128)(2,1)} %bitcast.14, bf16[4,2432,128]{2,1,0:T(8,128)(2,1)} %bitcast.11, bf16[2432,256]{1,0:T(8,128)(2,1)} %bitcast.13), custom_call_target="tpu_custom_call" | custom-call | tf_op jit(solution)/shard_map/analysis/pallas_call | solution.py:239
  24.2 1.9 %copy.8 = f32[256,38,16]{0,2,1:T(8,128)} copy(f32[256,38,16]{0,2,1:T(8,128)} %bitcast.12) | data formatting | bytes 1245184

commit v3 on v2

--- a/solution.py
+++ b/solution.py
@@ -39,6 +39,7 @@
     leaf_hbm,
     transfer_hbm,
     degree_hbm,
+    out_hbm,
     out_ref,
     grid_ref,
     leaf_ref,
@@ -53,6 +54,7 @@
     weight_sem,
     send_sem,
     recv_sem,
+    out_sem,
 ):
     orders, padded, rank, fields, cycles, nlon, levels, per_node, chunks, narrow = dims
     width = 2 * fields
@@ -125,7 +127,7 @@
         waves_ref[pl.ds(f, padded, stride=width), :] = flat[:padded] * scale
         waves_ref[pl.ds(fields + f, padded, stride=width), :] = flat[padded : 2 * padded] * scale
 
-    copies = []
+    copies, out_copies = [], []
 
     def send(b, g):
         mine = pl.ds(pl.multiple_of(uppers[b] * rank, rank), rank)
@@ -215,9 +217,15 @@
                     )
                     final = final[:width] + final[width:]
                     out_ref[o] = jnp.where(degree_id >= ids_ref[o], final, 0.0)
+                done = pl.ds(g * per_group, count)
+                copy = pltpu.make_async_copy(out_ref.at[done], out_hbm.at[done], out_sem.at[g])
+                copy.start()
+                out_copies.append(copy)
 
     for copy in copies:
         copy.wait_send()
+    for copy in out_copies:
+        copy.wait()
 
 
 def body(grid, cycle_weights, order_ids, leaf_weight, transfer, degree_weight):
@@ -240,8 +248,9 @@
         functools.partial(kernel, dims),
         out_shape=jax.ShapeDtypeStruct((orders, width, per_node), jnp.float32),
         in_specs=[smem, vmem, hbm, hbm, hbm, hbm],
-        out_specs=vmem,
+        out_specs=hbm,
         scratch_shapes=[
+            pltpu.VMEM((orders, width, per_node), jnp.float32),
             pltpu.VMEM((chunks, cycles * fields, nlon // chunks), jnp.bfloat16),
             pltpu.VMEM((orders * cycles, rank), jnp.bfloat16),
             pltpu.VMEM((levels, orders * rank, 2 * rank), jnp.bfloat16),
@@ -255,6 +264,7 @@
             pltpu.SemaphoreType.DMA((2 + levels,)),
             pltpu.SemaphoreType.DMA((levels, groups, 2)),
             pltpu.SemaphoreType.DMA((levels, groups, 2)),
+            pltpu.SemaphoreType.DMA((groups,)),
         ],
         compiler_params=pltpu.CompilerParams(
             collective_id=0, has_side_effects=True, vmem_limit_bytes=56 * 2**20

time: 26.3 us -> 26.1 us (level)
  no operation moved by 1% of the time
where the time goes in v3:
time: 26.1 us; the launch traced here: 25.9 us
  Pallas kernels  24 us (92%)
  local copies, waits for them, and re-layouts  1.94 us (7%)
    pallas_call x1, Pallas kernels, body(): pl.pallas_call(functools.partial(kernel, dims), out_shape=jax.ShapeDtypeS...  24 us
    unnamed x1, local copies, waits for them, and re-layouts  1.94 us

profile of v3, /device:TPU:0, one launch (start us, length us, event | category | flops | bytes accessed | tf_op | source)
XLA Modules:
  0.0 25.9 jit_solution(10103770868314402724)
XLA Ops:
  0.0 24.0 %analysis.1 = f32[38,16,256]{2,1,0:T(8,128)} custom-call(s32[38]{0:T(128)} %ids_ref.1, f32[1,64]{1,0:T(1,128)} %bitcast.15, bf16[512,8192]{1,0:T(8,128)(2,1)} %bitcast.10, bf16[2432,64]{1,0:T(8,128)(2,1)} %bitcast.14, bf16[4,2432,128]{2,1,0:T(8,128)(2,1)} %bitcast.11, bf16[2432,256]{1,0:T(8,128)(2,1)} %bitcast.13), custom_call_target="tpu_custom_call" | custom-call | tf_op jit(solution)/shard_map/analysis/pallas_call | solution.py:247
  24.0 1.9 %copy.8 = f32[256,38,16]{0,2,1:T(8,128)} copy(f32[256,38,16]{0,2,1:T(8,128)} %bitcast.12) | data formatting | bytes 1245184
